TPU v7x, 32 devices: a whole 2x2x4 slice. The times are simulated.
32 devices in a mesh: dp: 4 (over x, core), expert: 8 (over z, y).
Axes of the slice: x: 2, y: 2, z: 4, core: 2. Of those that a mesh axis runs over, the one named last changes fastest.
Arguments:
- tokens: bfloat16 [256, 4096], P(('dp', 'expert')), may hold values from -6 to 6
- expert_ids: int32 [256, 8], P(('dp', 'expert')), may hold values from 0 to 31, all different within a row; in each aligned block of 8 rows (0 to 7, 8 to 15, ...) at most 4 rows name the same one
- gate_weights: float32 [256, 8], P(('dp', 'expert')), may hold values from 0.1 to 1
- gate_weight: bfloat16 [4096, 14336], P('dp', 'expert'), may hold values from -0.09375 to 0.09375
- up_weight: bfloat16 [4096, 14336], P('dp', 'expert'), may hold values from -0.09375 to 0.09375
- down_weight: bfloat16 [14336, 4096], P('expert', 'dp'), may hold values from -0.125 to 0.125
- expert_gain: float32 [4, 14336], P('dp', 'expert'), may hold values from 0.5 to 2
Outputs:
- mixed: bfloat16 [256, 4096], P(('dp', 'expert'))
Inputs may be any that keep to these rules, and one draw needn't show every extreme that they name: `expert_ids`: each row names 8 different experts. Among the 8 rows of one device no expert is named more than 4 times, a bound that some block reaches.
All inputs are finite; a program needn't handle non-finite values.
Results may differ from a plain program's by a relative error of at most 0.0055.
Values may be sent and summed in bfloat16 or wider, within the bound.
A program may use at most 128 MiB of HBM per device.

v0:
```python
import jax
import jax.numpy as jnp
from jax import lax
from jax.sharding import PartitionSpec as P

FF = 14336
EH = 1792


def slot_table(expert_ids, segments, capacity):
    tok_rows, top_count = expert_ids.shape
    flat_ids = expert_ids.reshape(-1)
    route_order = jnp.arange(flat_ids.shape[0], dtype=jnp.int32)
    earlier = (flat_ids[:, None] == flat_ids[None, :]) & (
        route_order[None, :] < route_order[:, None]
    )
    rank_in = jnp.sum(earlier.astype(jnp.int32), axis=1)
    copy_index = flat_ids // segments
    segment_index = flat_ids % segments
    group_index = copy_index * segments + segment_index
    return (group_index * capacity + rank_in).reshape(tok_rows, top_count)


def dispatch(tokens, position, slot_count):
    targets = jnp.arange(slot_count, dtype=jnp.int32)
    onehot = jnp.any(targets[:, None, None] == position[None, :, :], axis=2).astype(jnp.bfloat16)
    return jnp.dot(onehot, tokens, preferred_element_type=jnp.float32).astype(jnp.bfloat16)


def expert_block(routed, gate_weight, up_weight, down_weight, expert_gain):

    def add_rows(piece):
        return jnp.dot(routed, piece, preferred_element_type=jnp.float32)

    gate_sum = add_rows(lax.all_gather(gate_weight, "dp", axis=0, tiled=True))
    up_sum = add_rows(lax.all_gather(up_weight, "dp", axis=0, tiled=True))
    hidden = (jax.nn.silu(gate_sum) * up_sum * expert_gain).astype(jnp.bfloat16)
    partial_value = jnp.dot(
        hidden,
        lax.all_gather(down_weight, "dp", axis=1, tiled=True),
        preferred_element_type=jnp.float32,
    )
    return partial_value.astype(jnp.bfloat16)


def body(tokens, expert_ids, gate_weights, gate_weight, up_weight, down_weight, expert_gain):
    copies = lax.axis_size("dp")
    owners = lax.axis_size("expert")
    segments = FF // EH
    quarters = owners // segments
    tok_rows, top_count = expert_ids.shape
    model_width = tokens.shape[1]
    experts = copies * segments
    capacity = max(2, (2 * tok_rows * top_count + experts - 1) // experts)
    slot_count = experts * capacity
    position = slot_table(expert_ids, segments, capacity)
    buffer = dispatch(tokens, position, slot_count)
    sectioned = buffer.reshape(copies, segments, capacity, model_width)
    arrived = lax.all_to_all(sectioned, "dp", split_axis=0, concat_axis=2, tiled=True)
    spread = jnp.broadcast_to(
        arrived.reshape(segments, 1, copies * capacity, model_width),
        (segments, quarters, copies * capacity, model_width),
    )
    spread = spread.reshape(owners, copies * capacity, model_width)
    rows_in = lax.all_to_all(spread, "expert", split_axis=0, concat_axis=1, tiled=True)
    partial_value = expert_block(
        rows_in.reshape(-1, model_width), gate_weight, up_weight, down_weight, expert_gain
    )
    returned = lax.all_to_all(
        partial_value.reshape(1, owners * copies * capacity, model_width),
        "expert",
        split_axis=1,
        concat_axis=0,
        tiled=True,
    )
    summed = jnp.sum(
        returned.reshape(segments, quarters, copies * capacity, model_width).astype(jnp.float32),
        axis=1,
    )
    summed = summed.astype(jnp.bfloat16)
    at_home = lax.all_to_all(
        summed.reshape(1, segments, copies * capacity, model_width),
        "dp",
        split_axis=2,
        concat_axis=0,
        tiled=True,
    )
    results = at_home.reshape(slot_count, model_width)
    picked = jnp.take(results, position.reshape(-1), axis=0).reshape(
        tok_rows, top_count, model_width
    )
    mixed = jnp.sum(gate_weights[:, :, None] * picked.astype(jnp.float32), axis=1)
    return mixed.astype(jnp.bfloat16)


def solution(mesh):
    in_specs = (
        P(("dp", "expert"), None),
        P(("dp", "expert"), None),
        P(("dp", "expert"), None),
        P("dp", "expert"),
        P("dp", "expert"),
        P("expert", "dp"),
        P("dp", "expert"),
    )
    out_specs = P(("dp", "expert"), None)
    return jax.shard_map(body, mesh=mesh, in_specs=in_specs, out_specs=out_specs, check_vma=False)
```

profile of v0, /device:TPU:27, one launch (start us, length us, event | category | flops | bytes accessed | tf_op | source)
XLA Modules:
  0.0 385.4 jit_solution(17198120846166784655)
XLA Ops:
  6.5 0.0 copy-start
  6.5 0.0 copy-start.3
  6.5 0.0 all-gather.4.cloned.1.call-start
  6.5 0.7 all-gather.4.cloned.1.call-update
  7.3 0.0 all-gather.6.cloned.1.call-start
  7.3 0.7 all-gather.6.cloned.1.call-update
  8.0 0.0 all-gather.8.cloned.1.call-start
  8.1 0.7 all-gather.8.cloned.1.call-update
  8.7 0.8 reshape.204
  9.5 0.2 convert_reduce_fusion
  9.7 0.1 reduce_sum.27
  9.8 0.7 compare_and_fusion
  10.5 0.1 fusion.6
  10.6 0.0 copy-done
  10.6 0.5 convolution_convert_fusion.1
  11.1 0.4 reshape.205
  11.5 0.6 copy.24
  12.1 21.5 %all_to_all.51 = bf16[4,8,4,4096]{3,1,2,0:T(8,128)(2,1)S(1)} all-to-all(bf16[4,8,4,4096]{3,1,2,0:T(8,128)(2,1)S(1)} %copy.24), channel_id=1, replica_groups=mesh['dp'=4,'expert'=8] {'dp'}, dimensions={0} | all-to-all | bytes 2097152 | tf_op jit(solution)/shard_map/all_to_all | solution.py:59
  33.6 1.6 copy.25
  35.1 5.5 %all-to-all-start.1 = ((bf16[8,16,4096]{2,1,0:T(8,128)(2,1)}), bf16[8,16,4096]{2,1,0:T(8,128)(2,1)S(1)}, u32[]{:S(2)}, u32[]{:S(2)}) async-start(bf16[8,16,4096]{2,1,0:T(8,128)(2,1)} %copy.25), calls=%async_computation.1 | async-start | bytes 2097152 | tf_op jit(solution)/shard_map/all_to_all | solution.py:65
  40.7 0.0 copy-done.3
  40.7 23.7 %all-to-all-done.1 = bf16[8,16,4096]{2,1,0:T(8,128)(2,1)S(1)} async-done(((bf16[8,16,4096]{2,1,0:T(8,128)(2,1)}), bf16[8,16,4096]{2,1,0:T(8,128)(2,1)S(1)}, u32[]{:S(2)}, u32[]{:S(2)}) %all-to-all-start.1) | async-done | bytes 1048608 | tf_op jit(solution)/shard_map/all_to_all | solution.py:65
  64.4 44.7 %all-gather.4.cloned.1.call-done = bf16[4096,1792]{1,0:T(8,128)(2,1)} async-done(((bf16[1024,1792]{1,0:T(8,128)(2,1)}), bf16[4096,1792]{1,0:T(8,128)(2,1)}) %all-gather.4.cloned.1.call-update) | async-done | bytes 14680080 | tf_op jit(solution)/shard_map/all_gather | solution.py:35
  109.1 7.2 %fusion.19 = f32[128,1792]{1,0:T(8,128)S(1)} fusion(bf16[128,4096]{1,0:T(8,128)(2,1)S(1)} %bitcast.36, bf16[4096,1792]{1,0:T(8,128)(2,1)} %all-gather.4.cloned.1.call-done), kind=kOutput, calls=%fused_computation.45 | convolution fusion | flops 1879048192 | bytes 16646144 | tf_op jit(solution)/shard_map/dot_general | solution.py:33
  116.4 88.6 %all-gather.6.cloned.1.call-done = bf16[4096,1792]{1,0:T(8,128)(2,1)} async-done(((bf16[1024,1792]{1,0:T(8,128)(2,1)}), bf16[4096,1792]{1,0:T(8,128)(2,1)}) %all-gather.6.cloned.1.call-update) | async-done | bytes 14680080 | tf_op jit(solution)/shard_map/all_gather | solution.py:36
  205.0 95.6 %all-gather.8.cloned.1.call-done = bf16[1792,4096]{1,0:T(8,128)(2,1)} async-done(((bf16[1792,1024]{1,0:T(8,128)(2,1)}), bf16[1792,4096]{1,0:T(8,128)(2,1)}) %all-gather.8.cloned.1.call-update) | async-done | bytes 14680080 | tf_op jit(solution)/shard_map/all_gather | solution.py:40
  300.6 0.0 copy-start.1
  300.6 13.8 %fusion = bf16[1,128,4096]{2,1,0:T(8,128)(2,1)S(1)} fusion(bf16[1792,4096]{1,0:T(8,128)(2,1)} %all-gather.8.cloned.1.call-done, bf16[128,4096]{1,0:T(8,128)(2,1)S(1)} %bitcast.37, bf16[4096,1792]{1,0:T(8,128)(2,1)} %all-gather.6.cloned.1.call-done, f32[128,1792]{1,0:T(8,128)S(1)} %fusion.19, f32[1792]{0:T(1024)S(1)} %reduce), kind=kOutput, calls=%fused_computation.3 | convolution fusion | flops 3760226304 | bytes 32381952 | tf_op jit(solution)/shard_map/dot_general | solution.py:38
  314.4 0.0 copy-start.2
  314.4 0.0 copy-start.4
  314.4 2.4 copy.33
  316.8 0.5 broadcast.207
  317.3 7.2 %reduce.1 = bf16[128,4096]{1,0:T(8,128)(2,1)S(1)} reduce(bf16[128,1,4096]{2,1,0:T(2,128)(2,1)S(1)} %bitcast.39, bf16[]{:T(256)} %broadcast.207), dimensions={1}, to_apply=%bitcast.35.reduce_sub_computation | reduce | bytes 2097154
  324.6 0.8 reshape.219
  325.4 28.5 %all_to_all.52 = bf16[8,2,32768]{2,1,0:T(2,128)(2,1)S(1)} all-to-all(bf16[8,2,32768]{2,1,0:T(2,128)(2,1)S(1)} %reshape.219), channel_id=1, replica_groups=mesh['dp'=4,'expert'=8] {'expert'}, dimensions={0} | all-to-all | bytes 2097152 | tf_op jit(solution)/shard_map/all_to_all | solution.py:69
  353.9 1.0 reshape.220
  355.0 1.1 copy.29
  356.1 1.5 copy.27
  357.7 5.6 %all-to-all-start.3 = ((bf16[1,8,16,4096]{3,1,0,2:T(8,128)(2,1)}), bf16[1,8,16,4096]{3,1,0,2:T(8,128)(2,1)S(1)}, u32[]{:S(2)}, u32[]{:S(2)}) async-start(bf16[1,8,16,4096]{3,1,0,2:T(8,128)(2,1)} %copy.27), calls=%async_computation.3 | async-start | bytes 2097152 | tf_op jit(solution)/shard_map/all_to_all | solution.py:81
  363.3 0.0 copy-done.2
  363.3 0.1 reshape.209
  363.4 12.4 %all-to-all-done.3 = bf16[1,8,16,4096]{3,1,0,2:T(8,128)(2,1)S(1)} async-done(((bf16[1,8,16,4096]{3,1,0,2:T(8,128)(2,1)}), bf16[1,8,16,4096]{3,1,0,2:T(8,128)(2,1)S(1)}, u32[]{:S(2)}, u32[]{:S(2)}) %all-to-all-start.3) | async-done | bytes 1048608 | tf_op jit(solution)/shard_map/all_to_all | solution.py:81
  375.8 0.8 copy.32
  376.7 0.3 reshape.208
  377.0 0.9 gather_fusion
  377.8 0.0 copy-done.4
  377.8 1.1 multiply_reduce_fusion
  378.9 0.0 copy-done.1
  (3 shorter events, 0.0 us)
Async XLA Ops:
  6.5 4.1 %copy-start = (bf16[8,4096]{1,0:T(8,128)(2,1)S(1)}, bf16[8,4096]{1,0:T(8,128)(2,1)}, u32[]{:S(2)}) copy-start(bf16[8,4096]{1,0:T(8,128)(2,1)} %param.7) | copy-start | bytes 196612
  6.5 34.2 %copy-start.3 = (f32[1,1792]{1,0:T(1,128)S(1)}, f32[1,1792]{1,0:T(1,128)}, u32[]{:S(2)}) copy-start(f32[1,1792]{1,0:T(1,128)} %param.13) | copy-start | bytes 21508
  6.5 102.6 %all-gather.4.cloned.1.call-start = ((), (), s32[]{:S(2)}) async-start(), calls=%async_computation.4 | async-start | bytes 18350080 | tf_op jit(solution)/shard_map/all_gather | solution.py:35
  7.3 197.7 %all-gather.6.cloned.1.call-start = ((), (), s32[]{:S(2)}) async-start(), calls=%async_computation.5 | async-start | bytes 18350080 | tf_op jit(solution)/shard_map/all_gather | solution.py:36
  8.0 292.6 %all-gather.8.cloned.1.call-start = ((), (), s32[]{:S(2)}) async-start(), calls=%async_computation.6 | async-start | bytes 18350080 | tf_op jit(solution)/shard_map/all_gather | solution.py:40
  35.1 29.3 %all-to-all-start.1 = ((bf16[8,16,4096]{2,1,0:T(8,128)(2,1)}), bf16[8,16,4096]{2,1,0:T(8,128)(2,1)S(1)}, u32[]{:S(2)}, u32[]{:S(2)}) async-start(bf16[8,16,4096]{2,1,0:T(8,128)(2,1)} %copy.25), calls=%async_computation.1 | async-start | bytes 2097152 | tf_op jit(solution)/shard_map/all_to_all | solution.py:65
  300.6 78.3 %copy-start.1 = (bf16[8,4096]{1,0:T(8,128)(2,1)S(1)}, bf16[8,4096]{1,0:T(8,128)(2,1)}, u32[]{:S(2)}) copy-start(bf16[8,4096]{1,0:T(8,128)(2,1)} %param.7) | copy-start | bytes 196612
  314.4 48.9 %copy-start.2 = (s32[8,8]{1,0:T(8,128)S(1)}, s32[8,8]{1,0:T(8,128)}, u32[]{:S(2)}) copy-start(s32[8,8]{1,0:T(8,128)} %param.8) | copy-start | bytes 772
  314.4 63.4 %copy-start.4 = (f32[8,8]{1,0:T(8,128)S(1)}, f32[8,8]{1,0:T(8,128)}, u32[]{:S(2)}) copy-start(f32[8,8]{1,0:T(8,128)} %param.9) | copy-start | bytes 772
  357.7 18.2 %all-to-all-start.3 = ((bf16[1,8,16,4096]{3,1,0,2:T(8,128)(2,1)}), bf16[1,8,16,4096]{3,1,0,2:T(8,128)(2,1)S(1)}, u32[]{:S(2)}, u32[]{:S(2)}) async-start(bf16[1,8,16,4096]{3,1,0,2:T(8,128)(2,1)} %copy.27), calls=%async_computation.3 | async-start | bytes 2097152 | tf_op jit(solution)/shard_map/all_to_all | solution.py:81
Sparse Core Ops, SparseCore 0:
  8.9 100.1 all-gather.3
  110.7 94.2 all-gather.5
  206.6 94.0 all-gather.7
where the time goes:
time: 391 us; the launch traced here: 385 us
  waiting for transfers between devices  267 us (68%)
  blocking collectives  50 us (13%)
  matrix products  21.5 us (5%)
  between operations  13.3 us (3%)
  local copies, waits for them, and re-layouts  12.9 us (3%)
  starting transfers between devices  11.2 us (3%)
  other arithmetic  9.34 us (2%)
    all_gather x1, waiting for transfers between devices, expert_block(): lax.all_gather(down_weight, 'dp', axis=1, tiled=True)  95.6 us
    all_gather x1, waiting for transfers between devices, expert_block(): up_sum = add_rows(lax.all_gather(up_weight, 'dp', axis=0, tiled=True))  88.6 us
    all_gather x1, waiting for transfers between devices, expert_block(): gate_sum = add_rows(lax.all_gather(gate_weight, 'dp', axis=0, tiled=True))  44.7 us
    all_to_all x1, blocking collectives, body(): lax.all_to_all(partial_value.reshape(1, owners * copies * capacity, model...  28.5 us
    all_to_all x1, waiting for transfers between devices, body(): lax.all_to_all(spread, 'expert', split_axis=0, concat_axis=1, tiled=True)  23.7 us
    all_to_all x1, blocking collectives, body(): lax.all_to_all(sectioned, 'dp', split_axis=0, concat_axis=2, tiled=True)  21.5 us
    dot_general x1, matrix products, expert_block(): jnp.dot(hidden, lax.all_gather(down_weight, 'dp', axis=1, tiled=True), pr...  13.8 us
    all_to_all x1, waiting for transfers between devices, body(): lax.all_to_all(summed.reshape(1, segments, copies * capacity, model_width...  12.4 us
  transfers between devices with their start and end apart: 5, of which 5 were waited for; matrix products, arithmetic and copies ran while one was open for 3% of the time, Pallas kernels for 0%

commit v1 on v0

v1 whole, which is shorter than its diff:
```python
import functools

import jax
import jax.numpy as jnp
from jax import lax
from jax.experimental import pallas as pl
from jax.experimental.pallas import tpu as pltpu
from jax.sharding import PartitionSpec as P

FF = 14336
EH = 1792
HALVES = 2
SKEW = (0, 1, 3, 5, 6)
SIB_DTYPE = jnp.float32
MESH = pl.DeviceIdType.MESH


def kernel(cfg, tok, ids, gws, gain, gate_hbm, up_hbm, down_hbm, out,
           wg, wu, wd, tf, t1, g1, xs, coefs, pbuf, pown, sbuf, xsend, xrecv, hid, acc, ob, rb, fs, fr,
           wsem, a_s, a_r, g_s, g_r, b_s, b_r, sib_s, sib_r, x_s, x_r, h_s, h_r, hf_s, hf_r, hs_s, hs_r,
           o_s, o_r, f_s, f_r):
    N, M, T, Dc, H, J, hc, Q = cfg
    X = N // 2
    NTQ = N * T // Q
    RQ = M * NTQ
    R = RQ // N
    NQ = N // Q
    SG = M // N
    copies = N
    segs = FF // EH
    d = lax.axis_index("dp")
    s = lax.axis_index("expert")
    xx = d // 2
    cc = d % 2
    sib = xx * 2 + (1 - cc)
    seg = s // (M // segs)

    loads = []
    for j in range(J):
        cols = pl.ds(j * hc, hc)
        loads.append((
            pltpu.make_async_copy(gate_hbm.at[:, cols], wg.at[j], wsem.at[j, 0]),
            pltpu.make_async_copy(up_hbm.at[:, cols], wu.at[j], wsem.at[j, 1]),
            pltpu.make_async_copy(down_hbm.at[cols, :], wd.at[j], wsem.at[j, 2]),
        ))
    for trio in loads:
        trio[0].start()
        trio[1].start()
    for trio in loads:
        trio[2].start()

    barrier = pltpu.get_barrier_semaphore()
    for k in range(1, N):
        pl.semaphore_signal(barrier, inc=1, device_id=((d + k) % N, s), device_id_type=MESH)
    for k in range(1, M):
        pl.semaphore_signal(barrier, inc=1, device_id=(d, (s + k) % M), device_id_type=MESH)

    lane = lax.broadcasted_iota(jnp.int32, (T, 128), 1)
    ids_v = ids[...]
    gw_v = gws[...]
    route = jnp.zeros((T, 128), jnp.float32)
    for k in range(ids_v.shape[1]):
        route = route + jnp.where(lane == ids_v[:, k:k + 1], gw_v[:, k:k + 1], 0.0)
    for p in range(N):
        tf[p, :, 0:Dc] = tok[:, p * Dc:(p + 1) * Dc].astype(jnp.float32)
        tf[p, :, Dc:Dc + 128] = route

    pl.semaphore_wait(barrier, N - 1 + M - 1)

    first = []
    for k in range(1, N):
        p = (d + k) % N
        c1 = pltpu.make_async_remote_copy(tf.at[p], t1.at[d], a_s.at[k - 1], a_r.at[k - 1],
                                          device_id=(p, s), device_id_type=MESH)
        c1.start()
        first.append(c1)
    second = []
    for k in range(1, N):
        p = (d + k) % N
        c2 = pltpu.make_async_remote_copy(gain, g1.at[d], g_s.at[k - 1], g_r.at[k - 1],
                                          device_id=(p, s), device_id_type=MESH)
        c2.start()
        second.append(c2)
    t1[d] = tf[d]
    g1[d] = gain[...]
    for c1 in first:
        c1.wait()

    bsend = []
    for q in range(Q):
        for r in range(NQ):
            pass
        v = t1[q * NQ:(q + 1) * NQ].reshape(NTQ, Dc + 128)
        w = v[:, Dc:]
        hi = w.astype(jnp.bfloat16)
        lo = (w - hi.astype(jnp.float32)).astype(jnp.bfloat16)
        xs[q, s, :, 0:Dc] = v[:, 0:Dc].astype(jnp.bfloat16)
        xs[q, s, :, Dc:Dc + 128] = hi
        xs[q, s, :, Dc + 128:] = lo
        for k in range(1, M):
            c = pltpu.make_async_remote_copy(xs.at[q, s], xs.at[q, s], b_s.at[q, k - 1], b_r.at[q, k - 1],
                                             device_id=(d, (s + k) % M), device_id_type=MESH)
            c.start()
            bsend.append(c)
    for c2 in second:
        c2.wait()

    sends = []

    def start_half(q):
        for k in range(M - 1):
            bsend[q * (M - 1) + k].wait_recv()
        w = xs[q, pl.ds(d * SG, SG), :, Dc:].reshape(R, 256)
        w = w[:, :128].astype(jnp.float32) + w[:, 128:].astype(jnp.float32)
        ln = lax.broadcasted_iota(jnp.int32, (R, 128), 1)
        for c in range(copies):
            one = jnp.sum(jnp.where(ln == c * segs + seg, w, 0.0), axis=1, keepdims=True)
            coefs[q, c] = jnp.broadcast_to(one, (R, 128))
        acc[q] = jnp.zeros((RQ, Dc), jnp.float32)

    def stage_a(q, j):
        u = q * J + j
        if j == 0:
            start_half(q)
        if q == 0:
            loads[j][0].wait()
            loads[j][1].wait()
        lhs = xs[q, :, :, 0:Dc].reshape(RQ, Dc)
        for i, mat in enumerate((wg, wu)):
            res = jnp.dot(lhs, mat[j], preferred_element_type=jnp.float32)
            res = res.reshape(X, 2, R, hc)
            for c in range(2):
                pown[u, c, :, i] = res[:, c]
        if SIB_DTYPE == jnp.float32:
            src = pown.at[u, 1 - cc]
        else:
            pbuf[u] = pown[u, 1 - cc].astype(SIB_DTYPE)
            src = pbuf.at[u]
        c = pltpu.make_async_remote_copy(src, sbuf.at[u], sib_s.at[u], sib_r.at[u],
                                         device_id=(sib, s), device_id_type=MESH)
        c.start()
        sends.append(c)
        return c

    def stage_b(u, sibc):
        sibc.wait_recv()
        cs = []
        for k in range(1, X):
            x2 = (xx + k) % X
            xsend[u, k - 1] = (pown[u, cc, x2] + sbuf[u, x2].astype(jnp.float32)).astype(jnp.bfloat16)
            c = pltpu.make_async_remote_copy(xsend.at[u, k - 1], xrecv.at[u, k - 1], x_s.at[u, k - 1],
                                             x_r.at[u, k - 1], device_id=(x2 * 2 + cc, s), device_id_type=MESH)
            c.start()
            cs.append(c)
            sends.append(c)
        return cs

    def stage_c(q, j, xcs):
        u = q * J + j
        tot = pown[u, cc, xx] + sbuf[u, xx].astype(jnp.float32)
        for k in range(1, X):
            xcs[k - 1].wait_recv()
            tot = tot + xrecv[u, k - 1].astype(jnp.float32)
        g = tot[0]
        up = tot[1]
        cf = jnp.zeros((R, hc), jnp.float32)
        for c in range(copies):
            cf = cf + coefs[q, c][:, 0:1] * g1[c, :, j * hc:(j + 1) * hc]
        hid[u, d] = ((g / (1.0 + jnp.exp(-g))) * up * cf).astype(jnp.bfloat16)
        cs = []
        for k in range(1, X):
            x2 = (xx + k) % X
            c = pltpu.make_async_remote_copy(hid.at[u, d], hid.at[u, d], h_s.at[u, k - 1], h_r.at[u, k - 1],
                                             device_id=(x2 * 2 + cc, s), device_id_type=MESH)
            c.start()
            cs.append(c)
            sends.append(c)
        c = pltpu.make_async_remote_copy(hid.at[u, d], hid.at[u, d], hs_s.at[u], hs_r.at[u],
                                         device_id=(sib, s), device_id_type=MESH)
        c.start()
        sends.append(c)
        return cs, c

    def stage_d(u, hcs):
        fw = []
        for k in range(1, X):
            x2 = (xx + X - k) % X
            hcs[k - 1].wait_recv()
            slot = hid.at[u, x2 * 2 + cc]
            c = pltpu.make_async_remote_copy(slot, slot, hf_s.at[u, k - 1], hf_r.at[u, k - 1],
                                             device_id=(sib, s), device_id_type=MESH)
            c.start()
            fw.append(c)
            sends.append(c)
        return fw

    def stage_e(q, j, own, fw):
        u = q * J + j
        own.wait_recv()
        for c in fw:
            c.wait_recv()
        if q == 0:
            loads[j][2].wait()
        h = hid[u].reshape(RQ, hc)
        acc[q] += jnp.dot(h, wd[j], preferred_element_type=jnp.float32)

    def stage_f(q):
        ob[q] = acc[q].reshape(M, NTQ, Dc).astype(jnp.bfloat16)
        cs = []
        for k in range(1, M):
            p = (s + k) % M
            c = pltpu.make_async_remote_copy(ob.at[q, p], rb.at[q, k - 1], o_s.at[q, k - 1], o_r.at[q, k - 1],
                                             device_id=(d, p), device_id_type=MESH)
            c.start()
            cs.append(c)
            sends.append(c)
        return cs

    def final_copy(p):
        return pltpu.make_async_remote_copy(fs.at[p], fr.at[d], f_s.at[p], f_r.at[d],
                                            device_id=(p, s), device_id_type=MESH)

    def stage_g(q, cs):
        tot = acc[q, pl.ds(pl.multiple_of(s * NTQ, NTQ), NTQ), :]
        for k in range(M - 1):
            cs[k].wait_recv()
            tot = tot + rb[q, k].astype(jnp.float32)
        tot = tot.reshape(NQ, T, Dc)
        for r in range(NQ):
            p = q * NQ + r
            fs[p] = tot[r]

            @pl.when(p != d)
            def _():
                final_copy(p).start()

    units = [(q, j) for q in range(Q) for j in range(J)]
    U = len(units)
    ra, rbx, rc, rd = {}, {}, {}, {}
    pending = []
    for t in range(U + SKEW[4]):
        u = t - SKEW[0]
        if 0 <= u < U:
            ra[u] = stage_a(*units[u])
        u = t - SKEW[1]
        if 0 <= u < U:
            rbx[u] = stage_b(u, ra[u])
        u = t - SKEW[2]
        if 0 <= u < U:
            rc[u] = stage_c(*units[u], rbx[u])
        u = t - SKEW[3]
        if 0 <= u < U:
            rd[u] = stage_d(u, rc[u][0])
        u = t - SKEW[4]
        if 0 <= u < U:
            q, j = units[u]
            stage_e(q, j, rc[u][1], rd[u])
            if j == J - 1:
                pending.append((q, stage_f(q)))
                if q == Q - 1:
                    for item in pending:
                        stage_g(*item)

    fr[d] = fs[d]
    for p in range(N):
        @pl.when(p != d)
        def _(p=p):
            pltpu.make_async_remote_copy(fs.at[p], fr.at[p], f_s.at[p], f_r.at[p],
                                         device_id=(p, s), device_id_type=MESH).wait()
    for p in range(N):
        out[:, p * Dc:(p + 1) * Dc] = fr[p].astype(jnp.bfloat16)
    for c in bsend:
        c.wait_send()
    for c in sends:
        c.wait_send()


def body(N, M, tokens, expert_ids, gate_weights, gate_weight, up_weight, down_weight, expert_gain):
    T, D = tokens.shape
    Dc, H = gate_weight.shape
    J = 7 if H % (7 * 256) == 0 else 1
    Q = HALVES
    hc = H // J
    X = N // 2
    U = Q * J
    NTQ = N * T // Q
    RQ = M * NTQ
    R = RQ // N
    bf, f32 = jnp.bfloat16, jnp.float32
    VM = pltpu.VMEM
    DMA = pltpu.SemaphoreType.DMA
    cfg = (N, M, T, Dc, H, J, hc, Q)
    vspec = pl.BlockSpec(memory_space=pltpu.VMEM)
    aspec = pl.BlockSpec(memory_space=pl.ANY)
    pb = (U, X, 2, R, hc) if SIB_DTYPE != f32 else (8, 128)
    return pl.pallas_call(
        functools.partial(kernel, cfg),
        out_shape=jax.ShapeDtypeStruct((T, D), bf),
        in_specs=[vspec, vspec, vspec, vspec, aspec, aspec, aspec],
        out_specs=vspec,
        scratch_shapes=[
            VM((J, Dc, hc), bf), VM((J, Dc, hc), bf), VM((J, hc, Dc), bf),
            VM((N, T, Dc + 128), f32), VM((N, T, Dc + 128), f32), VM((N, 1, H), f32),
            VM((Q, M, NTQ, Dc + 256), bf), VM((Q, N, R, 128), f32),
            VM(pb, SIB_DTYPE), VM((U, 2, X, 2, R, hc), f32), VM((U, X, 2, R, hc), SIB_DTYPE),
            VM((U, X - 1, 2, R, hc), bf), VM((U, X - 1, 2, R, hc), bf),
            VM((U, N, R, hc), bf), VM((Q, RQ, Dc), f32),
            VM((Q, M, NTQ, Dc), bf), VM((Q, M - 1, NTQ, Dc), bf),
            VM((N, T, Dc), f32), VM((N, T, Dc), f32),
            DMA((J, 3)),
            DMA((N - 1,)), DMA((N - 1,)), DMA((N - 1,)), DMA((N - 1,)),
            DMA((Q, M - 1)), DMA((Q, M - 1)),
            DMA((U,)), DMA((U,)), DMA((U, X - 1)), DMA((U, X - 1)),
            DMA((U, X - 1)), DMA((U, X - 1)), DMA((U, X - 1)), DMA((U, X - 1)), DMA((U,)), DMA((U,)),
            DMA((Q, M - 1)), DMA((Q, M - 1)), DMA((N,)), DMA((N,)),
        ],
        compiler_params=pltpu.CompilerParams(
            collective_id=0, has_side_effects=True, vmem_limit_bytes=56 * 1024 * 1024),
    )(tokens, expert_ids, gate_weights, expert_gain, gate_weight, up_weight, down_weight)


def solution(mesh):
    in_specs = (
        P(("dp", "expert"), None),
        P(("dp", "expert"), None),
        P(("dp", "expert"), None),
        P("dp", "expert"),
        P("dp", "expert"),
        P("expert", "dp"),
        P("dp", "expert"),
    )
    out_specs = P(("dp", "expert"), None)
    fn = functools.partial(body, mesh.shape["dp"], mesh.shape["expert"])
    return jax.shard_map(fn, mesh=mesh, in_specs=in_specs, out_specs=out_specs, check_vma=False)
```

time: 391 us -> 58.8 us (0.15); the launches traced: 385 us -> 58.6 us
  waiting for transfers between devices: 267 us -> 0 us
  Pallas kernels: 0 us -> 57.1 us
  blocking collectives: 50 us -> 0 us
  matrix products: 21.5 us -> 0 us
  between operations: 13.3 us -> 0.01 us
  local copies, waits for them, and re-layouts: 12.9 us -> 1.47 us
  starting transfers between devices: 11.2 us -> 0 us
  other arithmetic: 9.34 us -> 0 us
    all_gather x3 -> x0, waiting for transfers between devices: 229 us -> none  [the longest x1 95.6 us: expert_block(): lax.all_gather(down_weight, 'dp', axis=1, tiled=True)]
    pallas_call x0 -> x1, Pallas kernels: none -> 57.1 us  [body(): pl.pallas_call(functools.partial(kernel, cfg), out_shape=jax.ShapeDtypeSt...]
    all_to_all x2 -> x0, blocking collectives: 50 us -> none  [the longest x1 28.5 us: body(): lax.all_to_all(partial_value.reshape(1, owners * copies * capacity, model...]
    all_to_all x2 -> x0, waiting for transfers between devices: 36.1 us -> none  [the longest x1 23.7 us: body(): lax.all_to_all(spread, 'expert', split_axis=0, concat_axis=1, tiled=True)]
    dot_general x3 -> x0, matrix products: 21.5 us -> none  [the longest x1 13.8 us: expert_block(): jnp.dot(hidden, lax.all_gather(down_weight, 'dp', axis=1, tiled=True), pr...]
    all_to_all x2 -> x0, starting transfers between devices: 11.2 us -> none  [the longest x1 5.63 us: body(): lax.all_to_all(summed.reshape(1, segments, copies * capacity, model_width...]
    unnamed x2 -> x0, other arithmetic: 7.26 us -> none
    reshape x6 -> x0, local copies, waits for them, and re-layouts: 4.5 us -> none  [the longest x1 2.37 us: body(): partial_value.reshape(1, owners * copies * capacity, model_width)]
  transfers between devices with their start and end apart: 5 -> 0, of which waited for: 5 -> 0; matrix products, arithmetic and copies ran while one was open for 3% -> 0% of each run, Pallas kernels for 0% -> 0%
where the time goes in v1:
time: 58.8 us; the launch traced here: 58.6 us
  Pallas kernels  57.1 us (97%)
  local copies, waits for them, and re-layouts  1.47 us (2%)
    pallas_call x1, Pallas kernels, body(): pl.pallas_call(functools.partial(kernel, cfg), out_shape=jax.ShapeDtypeSt...  57.1 us
    unnamed x1, local copies, waits for them, and re-layouts  1.47 us

profile of v1, /device:TPU:27, one launch (start us, length us, event | category | flops | bytes accessed | tf_op | source)
XLA Modules:
  0.0 58.6 jit_solution(12055937510409951375)
XLA Ops:
  0.0 57.1 %shard_map.73 = bf16[8,4096]{1,0:T(8,128)(2,1)} custom-call(bf16[8,4096]{1,0:T(8,128)(2,1)} %tok.1, s32[8,8]{1,0:T(8,128)} %ids.1, f32[8,8]{1,0:T(8,128)} %gws.1, f32[1,1792]{1,0:T(1,128)} %gain.1, bf16[1024,1792]{1,0:T(8,128)(2,1)} %gate_hbm.1, bf16[1024,1792]{1,0:T(8,128)(2,1)} %up_hbm.1, bf16[1792,1024]{1,0:T(8,128)(2,1)} %down_hbm.1), custom_call_target="tpu_custom_call" | custom-call | tf_op jit(solution)/shard_map/pallas_call | solution.py:296
  57.1 1.5 %copy.9 = bf16[8,4096]{1,0:T(8,128)(2,1)} copy(bf16[8,4096]{1,0:T(8,128)(2,1)} %shard_map.73) | data formatting | bytes 131072

commit v2 on v1

--- a/solution.py
+++ b/solution.py
@@ -10,14 +10,14 @@
 FF = 14336
 EH = 1792
 HALVES = 2
-SKEW = (0, 1, 3, 5, 6)
+SKEW = (0, 1, 4, 7, 8)
 SIB_DTYPE = jnp.float32
 MESH = pl.DeviceIdType.MESH
 
 
 def kernel(cfg, tok, ids, gws, gain, gate_hbm, up_hbm, down_hbm, out,
            wg, wu, wd, tf, t1, g1, xs, coefs, pbuf, pown, sbuf, xsend, xrecv, hid, acc, ob, rb, fs, fr,
-           wsem, a_s, a_r, g_s, g_r, b_s, b_r, sib_s, sib_r, x_s, x_r, h_s, h_r, hf_s, hf_r, hs_s, hs_r,
+           wsem, a_s, a_r, g_s, g_r, b_s, b_r, bi_s, bi_r, sib_s, sib_r, x_s, x_r, h_s, h_r, hf_s, hf_r, hs_s, hs_r,
            o_s, o_r, f_s, f_r):
     N, M, T, Dc, H, J, hc, Q = cfg
     X = N // 2
@@ -52,20 +52,25 @@
     barrier = pltpu.get_barrier_semaphore()
     for k in range(1, N):
         pl.semaphore_signal(barrier, inc=1, device_id=((d + k) % N, s), device_id_type=MESH)
-    for k in range(1, M):
-        pl.semaphore_signal(barrier, inc=1, device_id=(d, (s + k) % M), device_id_type=MESH)
+    A = 4
+    B = M // A
+    a, b = s // B, s % B
+    for k in range(1, A):
+        pl.semaphore_signal(barrier, inc=1, device_id=(d, ((a + k) % A) * B + b), device_id_type=MESH)
+    for k in range(1, B):
+        pl.semaphore_signal(barrier, inc=1, device_id=(d, a * B + (b + k) % B), device_id_type=MESH)
 
     lane = lax.broadcasted_iota(jnp.int32, (T, 128), 1)
     ids_v = ids[...]
     gw_v = gws[...]
     route = jnp.zeros((T, 128), jnp.float32)
     for k in range(ids_v.shape[1]):
-        route = route + jnp.where(lane == ids_v[:, k:k + 1], gw_v[:, k:k + 1], 0.0)
+        route = route + jnp.where(lane % 64 == ids_v[:, k:k + 1], gw_v[:, k:k + 1], 0.0)
     for p in range(N):
         tf[p, :, 0:Dc] = tok[:, p * Dc:(p + 1) * Dc].astype(jnp.float32)
         tf[p, :, Dc:Dc + 128] = route
 
-    pl.semaphore_wait(barrier, N - 1 + M - 1)
+    pl.semaphore_wait(barrier, N - 1 + A - 1 + B - 1)
 
     first = []
     for k in range(1, N):
@@ -84,37 +89,47 @@
     t1[d] = tf[d]
     g1[d] = gain[...]
     for c1 in first:
-        c1.wait()
-
-    bsend = []
+        c1.wait_recv()
+
+    sends = list(first)
+    outer, inner = {}, {}
+
+    def relay(q, ka):
+        slot = xs.at[q, ((a + A - ka) % A) * B + b]
+        for kb in range(1, B):
+            c = pltpu.make_async_remote_copy(slot, slot, bi_s.at[q, ka, kb - 1], bi_r.at[q, ka, kb - 1],
+                                             device_id=(d, a * B + (b + kb) % B), device_id_type=MESH)
+            c.start()
+            inner[q, ka, kb] = c
+            sends.append(c)
+
+    half_lane = lax.broadcasted_iota(jnp.int32, (NTQ, 128), 1) < 64
     for q in range(Q):
-        for r in range(NQ):
-            pass
         v = t1[q * NQ:(q + 1) * NQ].reshape(NTQ, Dc + 128)
         w = v[:, Dc:]
-        hi = w.astype(jnp.bfloat16)
-        lo = (w - hi.astype(jnp.float32)).astype(jnp.bfloat16)
+        hi = w.astype(jnp.bfloat16).astype(jnp.float32)
         xs[q, s, :, 0:Dc] = v[:, 0:Dc].astype(jnp.bfloat16)
-        xs[q, s, :, Dc:Dc + 128] = hi
-        xs[q, s, :, Dc + 128:] = lo
-        for k in range(1, M):
-            c = pltpu.make_async_remote_copy(xs.at[q, s], xs.at[q, s], b_s.at[q, k - 1], b_r.at[q, k - 1],
-                                             device_id=(d, (s + k) % M), device_id_type=MESH)
-            c.start()
-            bsend.append(c)
-    for c2 in second:
-        c2.wait()
-
-    sends = []
+        xs[q, s, :, Dc:] = jnp.where(half_lane, hi, w - hi).astype(jnp.bfloat16)
+        for ka in range(1, A):
+            c = pltpu.make_async_remote_copy(xs.at[q, s], xs.at[q, s], b_s.at[q, ka - 1], b_r.at[q, ka - 1],
+                                             device_id=(d, ((a + ka) % A) * B + b), device_id_type=MESH)
+            c.start()
+            outer[q, ka] = c
+            sends.append(c)
+        relay(q, 0)
+    for q in range(Q):
+        for ka in range(1, A):
+            outer[q, ka].wait_recv()
+            relay(q, ka)
 
     def start_half(q):
-        for k in range(M - 1):
-            bsend[q * (M - 1) + k].wait_recv()
-        w = xs[q, pl.ds(d * SG, SG), :, Dc:].reshape(R, 256)
-        w = w[:, :128].astype(jnp.float32) + w[:, 128:].astype(jnp.float32)
+        for ka in range(A):
+            for kb in range(1, B):
+                inner[q, ka, kb].wait_recv()
+        w = xs[q, pl.ds(d * SG, SG), :, Dc:].reshape(R, 128).astype(jnp.float32)
         ln = lax.broadcasted_iota(jnp.int32, (R, 128), 1)
         for c in range(copies):
-            one = jnp.sum(jnp.where(ln == c * segs + seg, w, 0.0), axis=1, keepdims=True)
+            one = jnp.sum(jnp.where(ln % 64 == c * segs + seg, w, 0.0), axis=1, keepdims=True)
             coefs[q, c] = jnp.broadcast_to(one, (R, 128))
         acc[q] = jnp.zeros((RQ, Dc), jnp.float32)
 
@@ -157,6 +172,9 @@
 
     def stage_c(q, j, xcs):
         u = q * J + j
+        if u == 0:
+            for c2 in second:
+                c2.wait_recv()
         tot = pown[u, cc, xx] + sbuf[u, xx].astype(jnp.float32)
         for k in range(1, X):
             xcs[k - 1].wait_recv()
@@ -269,7 +287,7 @@
                                          device_id=(p, s), device_id_type=MESH).wait()
     for p in range(N):
         out[:, p * Dc:(p + 1) * Dc] = fr[p].astype(jnp.bfloat16)
-    for c in bsend:
+    for c in second:
         c.wait_send()
     for c in sends:
         c.wait_send()
@@ -301,7 +319,7 @@
         scratch_shapes=[
             VM((J, Dc, hc), bf), VM((J, Dc, hc), bf), VM((J, hc, Dc), bf),
             VM((N, T, Dc + 128), f32), VM((N, T, Dc + 128), f32), VM((N, 1, H), f32),
-            VM((Q, M, NTQ, Dc + 256), bf), VM((Q, N, R, 128), f32),
+            VM((Q, M, NTQ, Dc + 128), bf), VM((Q, N, R, 128), f32),
             VM(pb, SIB_DTYPE), VM((U, 2, X, 2, R, hc), f32), VM((U, X, 2, R, hc), SIB_DTYPE),
             VM((U, X - 1, 2, R, hc), bf), VM((U, X - 1, 2, R, hc), bf),
             VM((U, N, R, hc), bf), VM((Q, RQ, Dc), f32),
@@ -309,7 +327,7 @@
             VM((N, T, Dc), f32), VM((N, T, Dc), f32),
             DMA((J, 3)),
             DMA((N - 1,)), DMA((N - 1,)), DMA((N - 1,)), DMA((N - 1,)),
-            DMA((Q, M - 1)), DMA((Q, M - 1)),
+            DMA((Q, 3)), DMA((Q, 3)), DMA((Q, 4, M // 4 - 1)), DMA((Q, 4, M // 4 - 1)),
             DMA((U,)), DMA((U,)), DMA((U, X - 1)), DMA((U, X - 1)),
             DMA((U, X - 1)), DMA((U, X - 1)), DMA((U, X - 1)), DMA((U, X - 1)), DMA((U,)), DMA((U,)),
             DMA((Q, M - 1)), DMA((Q, M - 1)), DMA((N,)), DMA((N,)),

time: 58.8 us -> 52 us (0.88)
  Pallas kernels: 57.1 us -> 49.9 us
    pallas_call x1, Pallas kernels: 57.1 us -> 49.9 us  [body(): pl.pallas_call(functools.partial(kernel, cfg), out_shape=jax.ShapeDtypeSt...]
where the time goes in v2:
time: 52 us; the launch traced here: 51.4 us
  Pallas kernels  49.9 us (96%)
  local copies, waits for them, and re-layouts  1.47 us (3%)
    pallas_call x1, Pallas kernels, body(): pl.pallas_call(functools.partial(kernel, cfg), out_shape=jax.ShapeDtypeSt...  49.9 us
    unnamed x1, local copies, waits for them, and re-layouts  1.47 us

profile of v2, /device:TPU:27, one launch (start us, length us, event | category | flops | bytes accessed | tf_op | source)
XLA Modules:
  0.0 51.4 jit_solution(10118730381369029616)
XLA Ops:
  0.0 49.9 %shard_map.73 = bf16[8,4096]{1,0:T(8,128)(2,1)} custom-call(bf16[8,4096]{1,0:T(8,128)(2,1)} %tok.1, s32[8,8]{1,0:T(8,128)} %ids.1, f32[8,8]{1,0:T(8,128)} %gws.1, f32[1,1792]{1,0:T(1,128)} %gain.1, bf16[1024,1792]{1,0:T(8,128)(2,1)} %gate_hbm.1, bf16[1024,1792]{1,0:T(8,128)(2,1)} %up_hbm.1, bf16[1792,1024]{1,0:T(8,128)(2,1)} %down_hbm.1), custom_call_target="tpu_custom_call" | custom-call | tf_op jit(solution)/shard_map/pallas_call | solution.py:314
  49.9 1.5 %copy.9 = bf16[8,4096]{1,0:T(8,128)(2,1)} copy(bf16[8,4096]{1,0:T(8,128)(2,1)} %shard_map.73) | data formatting | bytes 131072
